TPU v7x, 512 devices: a whole 4x4x16 slice. The times are simulated.
512 devices in a mesh: row: 32 (over z_lo, x, core), col: 16 (over y, z_hi).
Axes of the slice: x: 4, y: 4, z: 16 (z_hi: 4, z_lo: 4; z = z_hi * 4 + z_lo), core: 2. Of those that a mesh axis runs over, the one named last changes fastest.
Arguments:
- acts: bfloat16 [2048, 16384], P('row', 'col'), may hold values from -6 to 6
- grads: float32 [16384, 512], P('col', 'row'), may hold values from -24 to 24
Outputs:
- factor: float32 [16384, 16384], P('row', 'col')
- applied: float32 [16384, 512], P('row', 'col')
- solution: float32 [16384, 512], P('col', 'row')
All inputs are finite; a program needn't handle non-finite values.
Results may differ from a plain program's by a relative error of at most 0.0003.
Values may be sent and summed in bfloat16 or wider, within the bound.
A program may use at most 64 MiB of HBM per device.

v0:
```python
import math

import jax
import jax.numpy as jnp
from jax import lax
from jax.sharding import Mesh
from jax.sharding import PartitionSpec as P

ROW = ("row_0", "row_1", "row_2")


damping = 1.0
highest = lax.Precision.HIGHEST


def in_order(pieces, dim):
    dims = list(pieces.shape[1:])
    dims[dim] *= pieces.shape[0]
    return jnp.moveaxis(pieces, 0, dim).reshape(dims)


def all_blocks(shard, axes, turns):
    pieces = shard[None]
    for k in turns:
        pieces = lax.all_gather(pieces, axes[k], axis=0, tiled=True)
    block = [lax.axis_size(axes[k]) for k in reversed(turns)]
    pieces = pieces.reshape(*block, *shard.shape)
    turned = sorted(range(len(turns)), key=lambda place: turns[len(turns) - 1 - place])
    return pieces.transpose(*turned, *range(len(turns), pieces.ndim)).reshape(-1, *shard.shape)


def gather_axes(shard, axes, turns, dim):
    return in_order(all_blocks(shard, axes, turns), dim)


def padded_to(lines, peers):
    spare = -lines.shape[0] % peers
    if not spare:
        return lines
    return jnp.concatenate([lines, jnp.zeros((spare, *lines.shape[1:]), lines.dtype)])


def from_root(shard, axis, root):
    lines = jnp.where(lax.axis_index(axis) == root, shard, jnp.zeros_like(shard)).reshape(
        -1, *shard.shape[1:][-1:]
    )
    padded = padded_to(lines, lax.axis_size(axis))
    own = lax.psum_scatter(padded, axis, scatter_dimension=0, tiled=True)
    return lax.all_gather(own, axis, axis=0, tiled=True)[: len(lines)].reshape(shard.shape)


def from_everyone(shard, axis):
    peers = lax.axis_size(axis)
    return lax.all_to_all(
        jnp.broadcast_to(shard[None], (peers, *shard.shape)), axis, 0, 0, tiled=True
    )


def gather_directly(shard, axis, dim):
    pieces = from_everyone(shard, axis)
    return in_order(pieces, dim)


def split_up(shard, dim, peers):
    before, after = (shard.shape[:dim], shard.shape[dim + 1 :])
    return jnp.moveaxis(shard.reshape(*before, peers, -1, *after), dim, 0)


def summed_on_arrival(shard, axis, dim):
    pieces = split_up(shard, dim, lax.axis_size(axis))
    arrived = lax.all_to_all(pieces, axis, split_axis=0, concat_axis=0, tiled=True)
    return arrived.sum(axis=0)


def step_size(feature_count, token_count):
    return 1.0 / (damping + (1.0 + math.sqrt(feature_count / token_count)) ** 2)


def local(acts, grads):
    row_count = lax.axis_size(ROW)
    col_count = lax.axis_size("col")
    row_ratio = row_count // col_count
    row_index = lax.axis_index(ROW)
    col_index = lax.axis_index("col")
    outer_width = acts.shape[1]
    inner_width = outer_width // row_ratio
    token_count = acts.shape[0] * row_count
    omega_step = step_size(outer_width * col_count, token_count)
    row_offset = row_index % row_ratio * inner_width
    owner_col = row_index // row_ratio
    column_panel = gather_axes(acts, ROW, (0, 1, 2), 0)
    owned_slice = lax.dynamic_slice_in_dim(column_panel, row_offset, inner_width, 1)
    inner_panel = from_root(owned_slice, "col", owner_col)
    gram_sum = lax.dot_general(
        inner_panel, column_panel, (((0,), (0,)), ((), ())), preferred_element_type=jnp.float32
    )
    gram_tile = gram_sum / token_count
    is_owner = (col_index == owner_col).astype(jnp.float32)
    gathered = gather_directly(grads, ROW, 1)
    mirror_rows = lax.dynamic_slice_in_dim(gathered, row_offset, inner_width, 0)
    partial_sum = jnp.dot(gram_tile, gathered, precision=highest) + damping * is_owner * mirror_rows
    applied = summed_on_arrival(partial_sum, "col", 1)
    full_applied = gather_directly(applied, "col", 1)
    mirror_coef = omega_step**3 * damping - 3.0 * omega_step**2
    empty_block = jnp.zeros((outer_width, full_applied.shape[1]), jnp.float32)
    placed = lax.dynamic_update_slice_in_dim(
        empty_block, full_applied * (mirror_coef * is_owner), row_offset, 0
    )
    second_sum = (
        omega_step**3
        * lax.dot_general(
            gram_tile,
            full_applied,
            (((0,), (0,)), ((), ())),
            precision=highest,
            preferred_element_type=jnp.float32,
        )
        + placed
    )
    solution = 3.0 * omega_step * grads + summed_on_arrival(second_sum, ROW, 1)
    return (gram_tile, applied, solution)


def solution(mesh):
    split = Mesh(
        mesh.devices.reshape(4, 4, 2, mesh.shape["col"]), ("row_0", "row_1", "row_2", "col")
    )
    in_specs = (P(ROW, "col"), P("col", ROW))
    out_specs = (P(ROW, "col"), P(ROW, "col"), P("col", ROW))
    return jax.shard_map(local, mesh=split, in_specs=in_specs, out_specs=out_specs, check_vma=False)
```

profile of v0, /device:TPU:6, one launch (start us, length us, event | category | flops | bytes accessed | tf_op | source)
XLA Modules:
  0.0 519.4 jit_solution(1728708824256396200)
XLA Ops:
  7.2 0.0 all-gather.5.cloned.1.call-start
  7.2 18.9 %all-gather = bf16[256,1024]{1,0:T(8,128)(2,1)} all-gather(bf16[64,1024]{1,0:T(8,128)(2,1)} %param.2), channel_id=2, replica_groups=mesh['row_0'=4,'row_1'=4,'row_2'=2,'col'=16] {'row_0'}, dimensions={0}, use_global_device_ids=true | all-gather | bytes 655360 | tf_op jit(solution)/shard_map/all_gather | solution.py:25
  26.1 0.0 all-gather.5.cloned.1.call-update
  26.2 0.0 all-gather.7.cloned.1.call-start
  26.2 38.5 %all-gather.5.cloned.1.call-done = bf16[16,64,1024]{2,1,0:T(8,128)(2,1)} async-done(((bf16[4,64,1024]{2,1,0:T(8,128)(2,1)}), bf16[16,64,1024]{2,1,0:T(8,128)(2,1)}) %all-gather.5.cloned.1.call-update) | async-done | bytes 2097168 | tf_op jit(solution)/shard_map/all_gather | solution.py:25
  64.7 0.0 all-gather.7.cloned.1.call-update
  64.7 0.0 reduce-scatter.2.cloned.1.call-start
  64.8 28.1 %all-gather.7.cloned.1.call-done = bf16[32,64,1024]{2,1,0:T(8,128)(2,1)} async-done(((bf16[16,64,1024]{2,1,0:T(8,128)(2,1)}), bf16[32,64,1024]{2,1,0:T(8,128)(2,1)}) %all-gather.7.cloned.1.call-update) | async-done | bytes 4194320 | tf_op jit(solution)/shard_map/all_gather | solution.py:25
  92.9 2.6 copy.6
  95.5 0.0 copy-start
  95.6 1.9 copy-done
  97.5 1.9 dynamic-slice_select_fusion
  99.4 0.0 copy-start.2
  99.4 0.0 reduce-scatter.2.cloned.1.call-update
  99.4 0.8 copy-done.2
  100.3 1.6 broadcast_in_dim.10
  101.9 8.0 %all-to-all-start = ((f32[32,1024,16]{1,2,0:T(8,128)}), f32[32,1024,16]{1,2,0:T(8,128)}, u32[]{:S(2)}, u32[]{:S(2)}) async-start(f32[32,1024,16]{1,2,0:T(8,128)} %broadcast_in_dim.10), calls=%async_computation.1 | async-start | bytes 4194304 | tf_op jit(solution)/shard_map/all_to_all | solution.py:54
  109.8 0.0 all-gather.9.cloned.1.call-start
  109.9 128.7 %reduce-scatter.2.cloned.1.call-done = bf16[128,512]{1,0:T(8,128)(2,1)} async-done(((bf16[2048,512]{1,0:T(8,128)(2,1)}), bf16[128,512]{1,0:T(8,128)(2,1)}) %reduce-scatter.2.cloned.1.call-update) | async-done | bytes 131088 | tf_op jit(solution)/shard_map/reduce_scatter | solution.py:48
  238.6 0.0 all-gather.9.cloned.1.call-update
  238.7 90.8 %all-gather.9.cloned.1.call-done = bf16[2048,512]{1,0:T(8,128)(2,1)} async-done(((bf16[128,512]{1,0:T(8,128)(2,1)}), bf16[2048,512]{1,0:T(8,128)(2,1)}) %all-gather.9.cloned.1.call-update) | async-done | bytes 2097168 | tf_op jit(solution)/shard_map/all_gather | solution.py:49
  329.5 5.2 convolution_multiply_fusion
  334.6 0.0 copy-start.1
  334.6 0.0 all-to-all-done
  334.7 6.2 %convolution_add_fusion = f32[512,512]{0,1:T(8,128)S(1)} fusion(f32[512,1024]{1,0:T(8,128)S(1)} %convolution_multiply_fusion, f32[1024,512]{0,1:T(8,128)} %bitcast.5, s32[]{:T(128)S(6)} %select_n.27, f32[]{:T(128)S(6)} %convert_element_type.3), kind=kOutput, calls=%fused_computation.3 | convolution fusion | flops 3221749760 | bytes 6291464 | tf_op jit(solution)/shard_map/dot_general | solution.py:101
  340.9 62.5 %all_to_all.20 = f32[16,512,32]{1,2,0:T(8,128)S(1)} all-to-all(f32[16,512,32]{1,2,0:T(8,128)S(1)} %bitcast.29), channel_id=1, replica_groups=mesh['row_0'=4,'row_1'=4,'row_2'=2,'col'=16] {'col'}, dimensions={0} | all-to-all | bytes 2097152 | tf_op jit(solution)/shard_map/all_to_all | solution.py:71
  403.4 0.1 reduce_sum.18
  403.4 0.0 copy-start.3
  403.5 1.1 broadcast_in_dim.22
  404.6 5.0 all-to-all-start.2
  409.6 45.6 %all-to-all-done.2 = f32[16,512,32]{1,2,0:T(8,128)S(1)} async-done(((f32[16,512,32]{1,2,0:T(8,128)}), f32[16,512,32]{1,2,0:T(8,128)S(1)}, u32[]{:S(2)}, u32[]{:S(2)}) %all-to-all-start.2) | async-done | bytes 1048608 | tf_op jit(solution)/shard_map/all_to_all | solution.py:54
  455.2 0.0 copy-done.1
  455.2 3.5 convolution_multiply_fusion.1
  458.8 0.0 copy-done.3
  458.8 0.3 add_dynamic-update-slice_fusion
  459.1 53.1 %all_to_all.21 = f32[32,1024,16]{1,2,0:T(8,128)S(1)} all-to-all(f32[32,1024,16]{1,2,0:T(8,128)S(1)} %bitcast.23), channel_id=1, replica_groups=mesh['row_0'=4,'row_1'=4,'row_2'=2,'col'=16] {'row_0','row_1','row_2'}, dimensions={0} | all-to-all | bytes 4194304 | tf_op jit(solution)/shard_map/all_to_all | solution.py:71
  512.1 0.1 reduce_sum.19
  512.3 0.6 multiply_add_fusion
Async XLA Ops:
  7.2 57.5 %all-gather.5.cloned.1.call-start = ((), (), s32[]{:S(2)}) async-start(), calls=%async_computation.5 | async-start | bytes 2621440 | tf_op jit(solution)/shard_map/all_gather | solution.py:25
  26.2 66.8 %all-gather.7.cloned.1.call-start = ((), (), s32[]{:S(2)}) async-start(), calls=%async_computation.6 | async-start | bytes 6291456 | tf_op jit(solution)/shard_map/all_gather | solution.py:25
  64.7 173.9 %reduce-scatter.2.cloned.1.call-start = ((), (), s32[]{:S(2)}) async-start(), calls=%async_computation.7 | async-start | bytes 2228224 | tf_op jit(solution)/shard_map/reduce_scatter | solution.py:48
  95.5 2.0 copy-start
  99.4 0.8 copy-start.2
  101.9 232.8 %all-to-all-start = ((f32[32,1024,16]{1,2,0:T(8,128)}), f32[32,1024,16]{1,2,0:T(8,128)}, u32[]{:S(2)}, u32[]{:S(2)}) async-start(f32[32,1024,16]{1,2,0:T(8,128)} %broadcast_in_dim.10), calls=%async_computation.1 | async-start | bytes 4194304 | tf_op jit(solution)/shard_map/all_to_all | solution.py:54
  109.8 219.6 %all-gather.9.cloned.1.call-start = ((), (), s32[]{:S(2)}) async-start(), calls=%async_computation.8 | async-start | bytes 2228224 | tf_op jit(solution)/shard_map/all_gather | solution.py:49
  334.6 120.6 %copy-start.1 = (f32[512,1024]{1,0:T(8,128)}, f32[512,1024]{1,0:T(8,128)S(1)}, u32[]{:S(2)}) copy-start(f32[512,1024]{1,0:T(8,128)S(1)} %convolution_multiply_fusion) | copy-start | bytes 6291460
  403.4 55.3 %copy-start.3 = (f32[512,32]{0,1:T(8,128)}, f32[512,32]{0,1:T(8,128)S(1)}, u32[]{:S(2)}) copy-start(f32[512,32]{0,1:T(8,128)S(1)} %reduce_sum.18) | copy-start | bytes 196612
  404.6 50.7 %all-to-all-start.2 = ((f32[16,512,32]{1,2,0:T(8,128)}), f32[16,512,32]{1,2,0:T(8,128)S(1)}, u32[]{:S(2)}, u32[]{:S(2)}) async-start(f32[16,512,32]{1,2,0:T(8,128)} %broadcast_in_dim.22), calls=%async_computation.3 | async-start | bytes 2097152 | tf_op jit(solution)/shard_map/all_to_all | solution.py:54
Sparse Core Ops, SparseCore 0:
  26.3 38.3 all-gather.4
  66.8 26.0 all-gather.6
  99.6 139.0 reduce-scatter.1
  241.9 87.4 all-gather.8
where the time goes:
time: 522 us; the launch traced here: 519 us
  waiting for transfers between devices  332 us (64%)
  blocking collectives  135 us (26%)
  matrix products  14.9 us (3%)
  between operations  13.9 us (3%)
  starting transfers between devices  13.2 us (3%)
  local copies, waits for them, and re-layouts  8.1 us (2%)
    reduce_scatter x1, waiting for transfers between devices, from_root(): own = lax.psum_scatter(padded, axis, scatter_dimension=0, tiled=True)  129 us
    all_to_all x2, blocking collectives, summed_on_arrival(): lax.all_to_all(pieces, axis, split_axis=0, concat_axis=0, tiled=True)  116 us
    all_gather x1, waiting for transfers between devices, from_root(): lax.all_gather(own, axis, axis=0, tiled=True)[:len(lines)]  90.8 us
    all_gather x2, waiting for transfers between devices, all_blocks(): pieces = lax.all_gather(pieces, axes[k], axis=0, tiled=True)  66.6 us
    all_to_all x2, waiting for transfers between devices, from_everyone(): lax.all_to_all(jnp.broadcast_to(shard[None], (peers, *shard.shape)), axis...  45.6 us
    all_gather x1, blocking collectives, all_blocks(): pieces = lax.all_gather(pieces, axes[k], axis=0, tiled=True)  18.9 us
    all_to_all x2, starting transfers between devices, from_everyone(): lax.all_to_all(jnp.broadcast_to(shard[None], (peers, *shard.shape)), axis...  13 us
  transfers between devices with their start and end apart: 6, of which 5 were waited for; matrix products, arithmetic and copies ran while one was open for 1% of the time, Pallas kernels for 0%

commit v1 on v0

v1 whole, which is shorter than its diff:
```python
import math

import jax
import jax.numpy as jnp
from jax import lax
from jax.experimental import pallas as pl
from jax.experimental.pallas import tpu as pltpu
from jax.sharding import Mesh
from jax.sharding import PartitionSpec as P

AXES = ("zl", "x", "core", "y", "zh")
ROW = ("zl", "x", "core")
COL = ("y", "zh")
DAMPING = 1.0
F32 = jnp.float32
BF16 = jnp.bfloat16


def step_size(feature_count, token_count):
    return 1.0 / (DAMPING + (1.0 + math.sqrt(feature_count / token_count)) ** 2)


def two_terms(v):
    hi = v.astype(BF16)
    lo = (v - hi.astype(F32)).astype(BF16)
    return jnp.concatenate([hi, lo], axis=0)


def folded(p):
    n = p.shape[0] // 2
    return p[:n] + p[n:]


def kernel(
    tokens, omega, acts, grads, f_out, ap_out, sol_out,
    AC, AK, LB, GH, AP, APH, YS, R1, S2, R2, R3, APS, APT,
    zl_s, zl_r, x_s, x_r, sib_s, sib_r, zs_s, zs_r, xs_s, p_r, ys_s, ys_r,
    rs_s, rs_r, zh_s, zh_r, ag_s, ag_r, ap_s, ap_r,
):
    zl, x, core, y, zh = [lax.axis_index(a) for a in AXES]
    sib = 1 - core

    def plus(v, d):
        return lax.rem(v + d, 4)

    def dev(zl_=zl, x_=x, core_=core, y_=y, zh_=zh):
        return (zl_, x_, core_, y_, zh_)

    def send(src, dst, ss, rs, to):
        pltpu.make_async_remote_copy(
            src_ref=src, dst_ref=dst, send_sem=ss, recv_sem=rs,
            device_id=to, device_id_type=pl.DeviceIdType.MESH,
        ).start()

    def wait(ref, sem):
        pltpu.make_async_copy(ref, ref, sem).wait()

    barrier = pltpu.get_barrier_semaphore()

    def hello(to):
        pl.semaphore_signal(barrier, inc=1, device_id=to, device_id_type=pl.DeviceIdType.MESH)

    on_line = zl == y
    diagonal = jnp.logical_and(x == zh, y == zl)
    for d in (1, 2, 3):
        hello(dev(zl_=plus(zl, d)))
        hello(dev(x_=plus(x, d)))
        hello(dev(y_=plus(y, d)))
        hello(dev(zh_=plus(zh, d)))
    hello(dev(core_=sib))
    for dz in range(4):
        for dl in range(4):
            for dc in range(2):
                to = dev(zl_=plus(zl, dl), core_=lax.rem(core + dc, 2), y_=zl, zh_=plus(zh, dz))
                if dz == dl == dc == 0:
                    pl.when(jnp.logical_not(on_line))(lambda to=to: hello(to))
                else:
                    hello(to)
    mirror = [dev(zl_=y, x_=zh, core_=lax.rem(core + dc, 2), y_=zl, zh_=x) for dc in range(2)]
    pl.when(jnp.logical_not(diagonal))(lambda: hello(mirror[0]))
    hello(mirror[1])

    g = jnp.transpose(grads[...])
    GH[...] = two_terms(g)
    AP[...] = g

    greeted = 13 + 31 + 1
    pl.semaphore_wait(barrier, greeted + jnp.where(on_line, 0, 1) + jnp.where(diagonal, 0, 1))

    def spot(dx, dl):
        return AC.at[:, plus(x, 4 - dx), plus(zl, 4 - dl) * 2 + core]

    def sib_spot(dx, dl):
        return AC.at[:, plus(x, 4 - dx), plus(zl, 4 - dl) * 2 + sib]

    def to_x(src, dl):
        for d in (1, 3, 2):
            send(src, spot(0, dl), x_s, x_r.at[d - 1, dl], dev(x_=plus(x, d)))

    def to_sib(src, dx, dl):
        send(src, spot(dx, dl), sib_s, sib_r.at[dx, dl], dev(core_=sib))

    own = pltpu.make_async_copy(acts, spot(0, 0), ap_s.at[2])
    own.start()
    for d in (1, 3, 2):
        send(acts, spot(0, 0), zl_s, zl_r.at[d - 1], dev(zl_=plus(zl, d)))
    to_sib(acts, 0, 0)
    to_x(acts, 0)
    for dz in (0, 1, 3, 2):
        for dy in range(4):
            for dc in range(2):
                part = plus(y, dy)
                half = lax.rem(core + dc, 2)
                src = acts.at[part, :, pl.ds(pl.multiple_of(half * 512, 512), 512)]
                dst = LB.at[zh, zl * 2 + core]
                to = dev(zl_=y, core_=half, y_=part, zh_=plus(zh, dz))
                if dz == dy == dc == 0:
                    @pl.when(on_line)
                    def _():
                        pltpu.make_async_copy(src, dst, zs_r.at[0]).start()

                    @pl.when(jnp.logical_not(on_line))
                    def _():
                        send(src, dst, zs_s.at[1], zs_r.at[0], to)
                else:
                    send(src, dst, zs_s.at[0 if dz == 0 else 2], zs_r.at[dz], to)

    def pass_on(dz):
        wait(LB.at[0], zs_r.at[dz])
        block = plus(zh, 4 - dz)

        @pl.when(block == x)
        def _():
            pltpu.make_async_copy(LB.at[block], AK.at[y, x], p_r.at[x]).start()

        @pl.when(block != x)
        def _():
            send(LB.at[block], AK.at[y, x], xs_s, p_r.at[x], dev(x_=block))

    def tokens_of(dq):
        return AC[:, plus(x, 4 - dq)].reshape(512, 1024)

    def partial(ph, q, rhs):
        a = tokens_of(q)
        p = folded(lax.dot_general(rhs[...], a, (((1,), (1,)), ((), ())), preferred_element_type=F32))
        for j in range(4):
            YS[ph, q, j] = p[:, 128 * j : 128 * (j + 1)]
        for d in (1, 3, 2):
            to = plus(y, d)
            send(YS.at[ph, q, to], R1.at[ph, q, d - 1], rs_s.at[ph], rs_r.at[ph, q, d - 1], dev(y_=to))

    def cross(ph, q):
        s = YS[ph, q, y]
        for d in (1, 3, 2):
            wait(R1.at[ph, q, d - 1], rs_r.at[ph, q, d - 1])
            s = s + R1[ph, q, d - 1]
        S2[ph, q] = s
        for d in (1, 3, 2):
            send(S2.at[ph, q], R2.at[ph, q, d - 1], zh_s.at[ph], zh_r.at[ph, q, d - 1], dev(zh_=plus(zh, d)))

    def spread(ph, q):
        s = S2[ph, q]
        for d in (1, 3, 2):
            wait(R2.at[ph, q, d - 1], zh_r.at[ph, q, d - 1])
            s = s + R2[ph, q, d - 1]
        R3[ph, q, y] = s
        for d in (1, 3, 2):
            send(R3.at[ph, q, y], R3.at[ph, q, y], ag_s.at[ph], ag_r.at[ph, q, d - 1], dev(y_=plus(y, d)))

    def collect(ph, q):
        for d in (1, 3, 2):
            wait(R3.at[ph, q, 0], ag_r.at[ph, q, d - 1])
        v = jnp.concatenate([R3[ph, q, j] for j in range(4)], axis=1)
        return folded(jnp.dot(two_terms(v), tokens_of(q), preferred_element_type=F32))

    def sib_quarter(dx):
        for dl in range(4):
            wait(sib_spot(dx, dl), sib_r.at[dx, dl])

    for d in (1, 3, 2):
        wait(spot(0, d), zl_r.at[d - 1])
        to_x(spot(0, d), d)
        to_sib(spot(0, d), 0, d)
    own.wait()
    pass_on(0)
    sib_quarter(0)
    partial(0, 0, GH)
    for dx in (1, 3):
        for dl in (0, 1, 3, 2):
            wait(spot(dx, dl), x_r.at[dx - 1, dl])
            to_sib(spot(dx, dl), dx, dl)
    pass_on(1)
    pass_on(3)
    cross(0, 0)
    sib_quarter(1)
    partial(0, 1, GH)
    sib_quarter(3)
    partial(0, 3, GH)
    for dl in (0, 1, 3, 2):
        wait(spot(2, dl), x_r.at[1, dl])
        to_sib(spot(2, dl), 2, dl)
    cross(0, 1)
    sib_quarter(2)
    partial(0, 2, GH)
    cross(0, 3)
    pass_on(2)
    cross(0, 2)
    spread(0, 0)
    for k in range(4):
        wait(AK.at[y, k], p_r.at[k])
        for d in (1, 3, 2):
            send(AK.at[y, k], AK.at[y, k], ys_s, ys_r.at[d - 1], dev(y_=plus(y, d)))
    for q in (1, 3, 2):
        spread(0, q)
    total = collect(0, 0)
    for q in (1, 3, 2):
        total = total + collect(0, q)
    applied = total * (1.0 / tokens) + DAMPING * g
    APH[...] = two_terms(applied)
    for h in range(2):
        APS[h] = applied[:, 512 * h : 512 * (h + 1)]
    for q in (0, 1, 3, 2):
        partial(1, q, APH)
    for dc in range(2):
        half = lax.rem(core + dc, 2)
        if dc == 0:
            @pl.when(diagonal)
            def _():
                pltpu.make_async_copy(APS.at[half], APT.at[core], ap_r.at[0]).start()

            @pl.when(jnp.logical_not(diagonal))
            def _():
                send(APS.at[half], APT.at[core], ap_s.at[0], ap_r.at[0], mirror[0])
        else:
            send(APS.at[half], APT.at[core], ap_s.at[1], ap_r.at[1], mirror[1])
    for q in (0, 1, 3, 2):
        cross(1, q)
    for d in (1, 3, 2):
        wait(AK.at[0], ys_r.at[d - 1])
    scale = 1.0 / tokens

    def tile(t, _):
        at = pl.ds(pl.multiple_of(t * 128, 128), 128)
        left = AK[:, :, :, :, at].reshape(2048, 128)
        right = AC[...].reshape(2048, 1024)
        f_out[at, :] = (
            lax.dot_general(left, right, (((0,), (0,)), ((), ())), preferred_element_type=F32) * scale
        )
        return 0

    lax.fori_loop(0, 4, tile, 0)
    for q in (0, 1, 3, 2):
        spread(1, q)
    total = collect(1, 0)
    for q in (1, 3, 2):
        total = total + collect(1, q)
    sol_out[...] = (
        3.0 * omega * g
        + (omega**3 * DAMPING - 3.0 * omega**2) * applied
        + (omega**3 / tokens) * total
    )
    wait(APT.at[0], ap_r.at[0])
    wait(APT.at[0], ap_r.at[1])
    ap_out[...] = APT[...].reshape(32, 512)

    wait(AC.at[:, 0, 0:3], zl_s)
    wait(AC.at[:, 0:3, 0:4], x_s)
    wait(AC.at[:, 0:2], sib_s)
    wait(LB.at[0, 0:7], zs_s.at[0])
    pl.when(jnp.logical_not(on_line))(lambda: wait(LB.at[0, 0], zs_s.at[1]))
    wait(LB.at[0:3], zs_s.at[2])
    wait(LB.at[0:3], xs_s)
    wait(AK.at[0:3], ys_s)
    for ph in range(2):
        wait(R1.at[ph], rs_s.at[ph])
        wait(R1.at[ph], zh_s.at[ph])
        wait(R1.at[ph], ag_s.at[ph])
    pl.when(jnp.logical_not(diagonal))(lambda: wait(APT.at[0], ap_s.at[0]))
    wait(APT.at[0], ap_s.at[1])


def local(acts, grads):
    tokens = 2048
    omega = step_size(16384, tokens)
    dma = pltpu.SemaphoreType.DMA
    vmem = pl.BlockSpec(memory_space=pltpu.VMEM)

    def body(*refs):
        kernel(tokens, omega, *refs)

    factor, ap, sol = pl.pallas_call(
        body,
        out_shape=(
            jax.ShapeDtypeStruct((512, 1024), F32),
            jax.ShapeDtypeStruct((32, 512), F32),
            jax.ShapeDtypeStruct((16, 1024), F32),
        ),
        in_specs=[vmem, vmem],
        out_specs=[vmem, vmem, vmem],
        scratch_shapes=[
            pltpu.VMEM((4, 4, 8, 16, 1024), BF16),
            pltpu.VMEM((4, 4, 8, 16, 512), BF16),
            pltpu.VMEM((4, 8, 16, 512), BF16),
            pltpu.VMEM((32, 1024), BF16),
            pltpu.VMEM((16, 1024), F32),
            pltpu.VMEM((32, 1024), BF16),
            pltpu.VMEM((2, 4, 4, 16, 128), F32),
            pltpu.VMEM((2, 4, 3, 16, 128), F32),
            pltpu.VMEM((2, 4, 16, 128), F32),
            pltpu.VMEM((2, 4, 3, 16, 128), F32),
            pltpu.VMEM((2, 4, 4, 16, 128), F32),
            pltpu.VMEM((2, 16, 512), F32),
            pltpu.VMEM((2, 16, 512), F32),
            dma(()), dma((3,)), dma(()), dma((3, 4)), dma(()), dma((4, 4)),
            dma((3,)), dma((4,)), dma(()), dma((4,)), dma(()), dma((3,)),
            dma((2,)), dma((2, 4, 3)), dma((2,)), dma((2, 4, 3)), dma((2,)), dma((2, 4, 3)),
            dma((3,)), dma((2,)),
        ],
        compiler_params=pltpu.CompilerParams(
            collective_id=0, has_side_effects=True, vmem_limit_bytes=48 * 2**20
        ),
        name="everything",
    )(acts.reshape(4, 16, 1024), grads)
    return factor, ap.T, sol.T


def solution(mesh):
    split = Mesh(mesh.devices.reshape(4, 4, 2, 4, 4), AXES)
    return jax.shard_map(
        local,
        mesh=split,
        in_specs=(P(ROW, COL), P(COL, ROW)),
        out_specs=(P(ROW, COL), P(ROW, COL), P(COL, ROW)),
        check_vma=False,
    )
```

time: 522 us -> 129 us (0.25)
  the two profiles are of different devices: /device:TPU:6 before, /device:TPU:44 now
where the time goes in v1:
time: 129 us; the launch traced here: 128 us
  Pallas kernels  123 us (95%)
  local copies, waits for them, and re-layouts  4.51 us (3%)
    pallas_call x1, Pallas kernels, local(): pl.pallas_call(body, out_shape=(jax.ShapeDtypeStruct((512, 1024), F32), j...  123 us
    unnamed x6, local copies, waits for them, and re-layouts  4.51 us

profile of v1, /device:TPU:44, one launch (start us, length us, event | category | flops | bytes accessed | tf_op | source)
XLA Modules:
  0.0 128.3 jit_solution(12941405177978873942)
XLA Ops:
  0.6 1.0 copy.5.refs_1_
  1.7 0.0 copy-start
  1.7 0.9 copy-done
  2.6 123.2 %everything.1 = (f32[512,1024]{1,0:T(8,128)S(1)}, f32[32,512]{1,0:T(8,128)S(1)}, f32[16,1024]{1,0:T(8,128)S(1)}) custom-call(bf16[4,16,1024]{2,1,0:T(8,128)(2,1)S(1)} %bitcast.3, f32[1024,16]{1,0:T(8,128)S(1)} %copy.5.refs_1_), custom_call_target="tpu_custom_call" | custom-call | tf_op jit(solution)/shard_map/everything/pallas_call | solution.py:291
  125.8 1.3 %copy.9 = f32[512,1024]{1,0:T(8,128)} copy(f32[512,1024]{1,0:T(8,128)S(1)} %get-tuple-element.12) | data formatting | bytes 4194304
  127.1 0.6 copy.10
  127.7 0.6 copy.11
Async XLA Ops:
  1.7 0.9 copy-start

commit v2 on v1

v2 whole, which is shorter than its diff:
```python
import math

import jax
import jax.numpy as jnp
from jax import lax
from jax.experimental import pallas as pl
from jax.experimental.pallas import tpu as pltpu
from jax.sharding import Mesh
from jax.sharding import PartitionSpec as P

AXES = ("zl", "x", "core", "y", "zh")
ROW = ("zl", "x", "core")
COL = ("y", "zh")
DAMPING = 1.0
F32 = jnp.float32
BF16 = jnp.bfloat16


def step_size(feature_count, token_count):
    return 1.0 / (DAMPING + (1.0 + math.sqrt(feature_count / token_count)) ** 2)


def two_terms(v):
    hi = v.astype(BF16)
    lo = (v - hi.astype(F32)).astype(BF16)
    return jnp.concatenate([hi, lo], axis=0)


def folded(p):
    n = p.shape[0] // 2
    return p[:n] + p[n:]


def kernel(
    tokens, omega, acts, grads, f_out, ap_out, sol_out,
    AC, AK, LB, SC, GX, APH, YA, YP, P1, P2, P3, P4, YS, R1, S2, R2, R3, APS, APT,
    sc_s, sc_r, zl_s, zl_r, x_s, x_r, sib_s, sib_r, zs_s, zs_r, xs_s, p_r, ys_s, ys_r,
    gx_s, gx_r, p1_s, p1_r, p2_s, p2_r, ya_s, ya_r, rs_s, rs_r, zh_s, zh_r, ag_s, ag_r, ap_s, ap_r,
):
    zl, x, core, y, zh = [lax.axis_index(a) for a in AXES]
    sib = 1 - core

    def plus(v, d):
        return lax.rem(v + d, 4)

    def dev(zl_=zl, x_=x, core_=core, y_=y, zh_=zh):
        return (zl_, x_, core_, y_, zh_)

    def send(src, dst, ss, rs, to):
        pltpu.make_async_remote_copy(
            src_ref=src, dst_ref=dst, send_sem=ss, recv_sem=rs,
            device_id=to, device_id_type=pl.DeviceIdType.MESH,
        ).start()

    def wait(ref, sem):
        pltpu.make_async_copy(ref, ref, sem).wait()

    barrier = pltpu.get_barrier_semaphore()

    def hello(to):
        pl.semaphore_signal(barrier, inc=1, device_id=to, device_id_type=pl.DeviceIdType.MESH)

    diagonal = jnp.logical_and(x == zh, y == zl)
    for d in (1, 2, 3):
        hello(dev(zl_=plus(zl, d)))
        hello(dev(x_=plus(x, d)))
        hello(dev(y_=plus(y, d)))
        hello(dev(zh_=plus(zh, d)))
        for e in (1, 2, 3):
            hello(dev(x_=plus(x, d), y_=plus(y, e)))
        hello(dev(core_=sib, y_=plus(y, d)))
    hello(dev(core_=sib))
    for dz in range(4):
        for dl in range(4):
            if dz and dl:
                hello(dev(zl_=plus(zl, dl), zh_=plus(zh, dz)))
    mirror = [dev(zl_=y, x_=zh, core_=lax.rem(core + dc, 2), y_=zl, zh_=x) for dc in range(2)]
    pl.when(jnp.logical_not(diagonal))(lambda: hello(mirror[0]))
    hello(mirror[1])

    g = jnp.transpose(grads[...])
    GX[x] = two_terms(g)

    greeted = 13 + 9 + 3 + 9 + 1
    pl.semaphore_wait(barrier, greeted + jnp.where(diagonal, 0, 1))

    def spot(dx, dl):
        return AC.at[plus(x, 4 - dx), plus(zl, 4 - dl), :, core]

    def sib_spot(dx, dl):
        return AC.at[plus(x, 4 - dx), plus(zl, 4 - dl), :, sib]

    def to_x(src, dl):
        for d in (1, 3):
            send(src, spot(0, dl), x_s, x_r.at[d - 1, dl], dev(x_=plus(x, d)))

    def to_sib(src, dx, dl):
        send(src, spot(dx, dl), sib_s, sib_r.at[dx, dl], dev(core_=sib))

    def scatter():
        for dy in (1, 3, 2, 0):
            for dc in range(2):
                part, half = plus(y, dy), lax.rem(core + dc, 2)
                src = acts.at[part, :, pl.ds(pl.multiple_of(half * 512, 512), 512)]
                dst = SC.at[y, core]
                if dy or dc:
                    send(src, dst, sc_s, sc_r, dev(core_=half, y_=part))
                else:
                    pltpu.make_async_copy(src, dst, sc_r).start()

    def over_z(dz):
        dst = LB.at[zh, pl.ds(zl * 2, 2)]
        for dl in (1, 3, 2, 0):
            at = plus(zl, dl)
            if dz or dl:
                send(SC.at[at], dst, zs_s.at[0 if dz == 0 else 1], zs_r.at[dz], dev(zl_=at, zh_=plus(zh, dz)))
            else:
                pltpu.make_async_copy(SC.at[at], dst, zs_r.at[0]).start()

    def pass_on(dz):
        wait(LB.at[0], zs_r.at[dz])
        block = plus(zh, 4 - dz)

        @pl.when(block == x)
        def _():
            pltpu.make_async_copy(LB.at[block], AK.at[y, x], p_r.at[x]).start()

        @pl.when(block != x)
        def _():
            send(LB.at[block], AK.at[y, x], xs_s, p_r.at[x], dev(x_=block))

    def over_y(dz):
        @pl.when(plus(zh, 4 - dz) == x)
        def _():
            for k in range(4):
                wait(AK.at[y, k], p_r.at[k])
                for d in (1, 3):
                    send(AK.at[y, k], AK.at[y, k], ys_s, ys_r.at[d - 1, k], dev(y_=plus(y, d)))

    def wait_y(n, k):
        wait(AK.at[0, 0], ys_r.at[n - 1, k])

    def relay_y():
        for k in range(4):
            d = 1 if k < 2 else 3
            at = AK.at[plus(y, 4 - d), k]
            wait_y(d, k)
            send(at, at, ys_s, ys_r.at[1, k], dev(y_=plus(y, d)))

    def first_partial(dl):
        j = plus(zl, 4 - dl)
        a = AC[x, j].reshape(128, 1024)
        p = lax.dot_general(
            GX[...].reshape(128, 1024), a, (((1,), (1,)), ((), ())), preferred_element_type=F32
        ).reshape(4, 2, 16, 128)
        YP[j] = p[:, 0] + p[:, 1]

        @pl.when(j != y)
        def _():
            send(YP.at[j], P1.at[y], p1_s, p1_r.at[y], dev(y_=j))

    def first_cross():
        v = YP[y]
        for d in (1, 3, 2):
            at = plus(y, d)
            wait(P1.at[at], p1_r.at[at])
            v = v + P1[at]
        P2[...] = v
        for d in (2, 1, 3):
            send(P2, P3.at[d - 1], p2_s, p2_r.at[d - 1], dev(zh_=plus(zh, d)))

    def first_spread():
        v = P2[...]
        for d in (1, 3, 2):
            wait(P3.at[d - 1], p2_r.at[d - 1])
            v = v + P3[d - 1]
        P4[...] = v
        YA[x, y] = P4[x]
        for dx in (0, 1, 3, 2):
            for dy in (0, 1, 3, 2):
                if dx or dy:
                    xt = plus(x, dx)
                    send(P4.at[xt], YA.at[x, y], ya_s.at[1 if dx == 0 else 0], ya_r.at[dx, dy], dev(x_=xt, y_=plus(y, dy)))

    def product(pieces, q):
        v = jnp.concatenate(pieces, axis=1)
        a = AC[plus(x, 4 - q)].reshape(512, 1024)
        return folded(jnp.dot(two_terms(v), a, preferred_element_type=F32))

    def first_collect(q):
        for d in (0, 1, 3, 2):
            if q or d:
                wait(YA.at[0, 0], ya_r.at[q, d])
        xq = plus(x, 4 - q)
        return product([YA[xq, j] for j in range(4)], q)

    def partial(q):
        a = AC[plus(x, 4 - q)].reshape(512, 1024)
        p = folded(lax.dot_general(APH[...], a, (((1,), (1,)), ((), ())), preferred_element_type=F32))
        for j in range(4):
            YS[q, j] = p[:, 128 * j : 128 * (j + 1)]
        for d in (1, 3, 2):
            to = plus(y, d)
            send(YS.at[q, to], R1.at[q, d - 1], rs_s, rs_r.at[q, d - 1], dev(y_=to))

    def cross(q):
        v = YS[q, y]
        for d in (1, 3, 2):
            wait(R1.at[q, d - 1], rs_r.at[q, d - 1])
            v = v + R1[q, d - 1]
        S2[q] = v
        for d in (2, 1, 3):
            send(S2.at[q], R2.at[q, d - 1], zh_s, zh_r.at[q, d - 1], dev(zh_=plus(zh, d)))

    def spread(q):
        v = S2[q]
        for d in (1, 3, 2):
            wait(R2.at[q, d - 1], zh_r.at[q, d - 1])
            v = v + R2[q, d - 1]
        R3[q, y] = v
        for d in (1, 3, 2):
            send(R3.at[q, y], R3.at[q, y], ag_s, ag_r.at[q, d - 1], dev(y_=plus(y, d)))

    def collect(q):
        for d in (1, 3, 2):
            wait(R3.at[q, 0], ag_r.at[q, d - 1])
        return product([R3[q, j] for j in range(4)], q)

    def sib_quarter(dx):
        for dl in range(4):
            wait(sib_spot(dx, dl), sib_r.at[dx, dl])

    scale = 1.0 / tokens

    def factor_part(n):
        i = plus(y, 4 - n)

        def tile(t, _):
            at = pl.ds(pl.multiple_of(t * 128, 128), 128)
            left = AK[i, :, :, :, at].reshape(512, 128)
            right = AC[:, :, i].reshape(512, 1024)
            p = lax.dot_general(left, right, (((0,), (0,)), ((), ())), preferred_element_type=F32) * scale
            f_out[at, :] = p if n == 0 else f_out[at, :] + p
            return 0

        lax.fori_loop(0, 4, tile, 0)

    scatter()
    own = pltpu.make_async_copy(acts, spot(0, 0), ap_s.at[2])
    own.start()
    for d in (1, 3, 2):
        send(acts, spot(0, 0), zl_s, zl_r.at[d - 1], dev(zl_=plus(zl, d)))
    to_sib(acts, 0, 0)
    for d in (1, 3, 2):
        send(GX.at[x], GX.at[x], gx_s, gx_r.at[d - 1], dev(x_=plus(x, d)))
    to_x(acts, 0)
    for d in (1, 3, 2):
        wait(spot(0, d), zl_r.at[d - 1])
        to_x(spot(0, d), d)
        to_sib(spot(0, d), 0, d)
        if d == 1:
            own.wait()
            for e in (1, 3, 2):
                wait(GX.at[0], gx_r.at[e - 1])
            wait(sib_spot(0, 0), sib_r.at[0, 0])
            first_partial(0)
    for d in (1, 3, 2):
        wait(sib_spot(0, d), sib_r.at[0, d])
        first_partial(d)
    first_cross()
    wait(SC, sc_r)
    over_z(2)
    over_z(1)
    over_z(3)
    over_z(0)
    for dl in (0, 1, 3, 2):
        for dx in (1, 3):
            wait(spot(dx, dl), x_r.at[dx - 1, dl])
            if (dx == 1) == (dl < 2):
                send(spot(dx, dl), spot(dx, dl), x_s, x_r.at[1, dl], dev(x_=plus(x, dx)))
            to_sib(spot(dx, dl), dx, dl)
    first_spread()
    for dl in (0, 1, 3, 2):
        wait(spot(2, dl), x_r.at[1, dl])
        to_sib(spot(2, dl), 2, dl)
    pass_on(2)
    total = first_collect(0)
    for q in (1, 3, 2):
        sib_quarter(q)
        total = total + first_collect(q)
    applied = total * scale + DAMPING * g
    APH[...] = two_terms(applied)
    for h in range(2):
        APS[h] = applied[:, 512 * h : 512 * (h + 1)]
    for q in (0, 1, 3, 2):
        partial(q)
    pass_on(1)
    pass_on(3)
    pass_on(0)
    for q in (0, 1, 3, 2):
        cross(q)
    for dc in range(2):
        half = lax.rem(core + dc, 2)
        if dc == 0:
            @pl.when(diagonal)
            def _():
                pltpu.make_async_copy(APS.at[half], APT.at[core], ap_r.at[0]).start()

            @pl.when(jnp.logical_not(diagonal))
            def _():
                send(APS.at[half], APT.at[core], ap_s.at[0], ap_r.at[0], mirror[0])
        else:
            send(APS.at[half], APT.at[core], ap_s.at[1], ap_r.at[1], mirror[1])
    over_y(2)
    over_y(1)
    over_y(3)
    over_y(0)
    for q in (0, 1, 3, 2):
        spread(q)
    relay_y()
    factor_part(0)
    total = collect(0)
    for q in (1, 3, 2):
        total = total + collect(q)
    sol_out[...] = (
        3.0 * omega * g
        + (omega**3 * DAMPING - 3.0 * omega**2) * applied
        + (omega**3 / tokens) * total
    )
    wait(APT.at[0], ap_r.at[0])
    wait(APT.at[0], ap_r.at[1])
    ap_out[...] = APT[...].reshape(32, 512)
    for n in (1, 3, 2):
        for k in range(4):
            if n != 2 and (n == 1) == (k < 2):
                continue
            wait_y(n, k)
        factor_part(n)

    wait(AC.at[0:3, 0, :, 0], zl_s)
    wait(AC.at[0:3, :, :, 0], x_s)
    wait(AC.at[:, :, :, 0], sib_s)
    wait(LB.at[0, 0:7], sc_s)
    wait(LB.at[0, 0:6], zs_s.at[0])
    wait(LB.at[0:3], zs_s.at[1])
    wait(LB.at[0:3], xs_s)
    wait(AK.at[0:3], ys_s)
    wait(GX.at[0:3], gx_s)
    wait(P1.at[0:3], p1_s)
    wait(P3, p2_s)
    wait(YA.at[0:3], ya_s.at[0])
    wait(YA.at[0, 0:3], ya_s.at[1])
    wait(R1, rs_s)
    wait(R1, zh_s)
    wait(R1, ag_s)
    pl.when(jnp.logical_not(diagonal))(lambda: wait(APT.at[0], ap_s.at[0]))
    wait(APT.at[0], ap_s.at[1])


def local(acts, grads):
    tokens = 2048
    omega = step_size(16384, tokens)
    dma = pltpu.SemaphoreType.DMA
    vmem = pl.BlockSpec(memory_space=pltpu.VMEM)

    def body(*refs):
        kernel(tokens, omega, *refs)

    factor, ap, sol = pl.pallas_call(
        body,
        out_shape=(
            jax.ShapeDtypeStruct((512, 1024), F32),
            jax.ShapeDtypeStruct((32, 512), F32),
            jax.ShapeDtypeStruct((16, 1024), F32),
        ),
        in_specs=[vmem, vmem],
        out_specs=[vmem, vmem, vmem],
        scratch_shapes=[
            pltpu.VMEM((4, 4, 4, 2, 16, 1024), BF16),
            pltpu.VMEM((4, 4, 8, 16, 512), BF16),
            pltpu.VMEM((4, 8, 16, 512), BF16),
            pltpu.VMEM((4, 2, 16, 512), BF16),
            pltpu.VMEM((4, 32, 1024), BF16),
            pltpu.VMEM((32, 1024), BF16),
            pltpu.VMEM((4, 4, 16, 128), F32),
            pltpu.VMEM((4, 4, 16, 128), F32),
            pltpu.VMEM((4, 4, 16, 128), F32),
            pltpu.VMEM((4, 16, 128), F32),
            pltpu.VMEM((3, 4, 16, 128), F32),
            pltpu.VMEM((4, 16, 128), F32),
            pltpu.VMEM((4, 4, 16, 128), F32),
            pltpu.VMEM((4, 3, 16, 128), F32),
            pltpu.VMEM((4, 16, 128), F32),
            pltpu.VMEM((4, 3, 16, 128), F32),
            pltpu.VMEM((4, 4, 16, 128), F32),
            pltpu.VMEM((2, 16, 512), F32),
            pltpu.VMEM((2, 16, 512), F32),
            dma(()), dma(()), dma(()), dma((3,)), dma(()), dma((3, 4)), dma(()), dma((4, 4)),
            dma((2,)), dma((4,)), dma(()), dma((4,)), dma(()), dma((3, 4)),
            dma(()), dma((3,)), dma(()), dma((4,)), dma(()), dma((3,)), dma((2,)), dma((4, 4)),
            dma(()), dma((4, 3)), dma(()), dma((4, 3)), dma(()), dma((4, 3)),
            dma((3,)), dma((2,)),
        ],
        compiler_params=pltpu.CompilerParams(
            collective_id=0, has_side_effects=True, vmem_limit_bytes=48 * 2**20
        ),
        name="everything",
    )(acts.reshape(4, 16, 1024), grads)
    return factor, ap.T, sol.T


def solution(mesh):
    split = Mesh(mesh.devices.reshape(4, 4, 2, 4, 4), AXES)
    return jax.shard_map(
        local,
        mesh=split,
        in_specs=(P(ROW, COL), P(COL, ROW)),
        out_specs=(P(ROW, COL), P(ROW, COL), P(COL, ROW)),
        check_vma=False,
    )
```

time: 129 us -> 96.8 us (0.75)
  the two profiles are of different devices: /device:TPU:44 before, /device:TPU:6 now
where the time goes in v2:
time: 96.8 us; the launch traced here: 95.5 us
  Pallas kernels  90.3 us (93%)
  local copies, waits for them, and re-layouts  4.51 us (5%)
    pallas_call x1, Pallas kernels, local(): pl.pallas_call(body, out_shape=(jax.ShapeDtypeStruct((512, 1024), F32), j...  90.3 us
    unnamed x6, local copies, waits for them, and re-layouts  4.51 us

profile of v2, /device:TPU:6, one launch (start us, length us, event | category | flops | bytes accessed | tf_op | source)
XLA Modules:
  0.0 95.5 jit_solution(5098351407623914943)
XLA Ops:
  0.6 1.0 %copy.5.refs_1_ = f32[1024,16]{1,0:T(8,128)S(1)} copy(f32[1024,16]{0,1:T(8,128)} %param.3) | data formatting | bytes 131072 | tf_op args[1]
  1.7 0.0 copy-start
  1.7 0.9 copy-done
  2.6 90.3 %everything.1 = (f32[512,1024]{1,0:T(8,128)S(1)}, f32[32,512]{1,0:T(8,128)S(1)}, f32[16,1024]{1,0:T(8,128)S(1)}) custom-call(bf16[4,16,1024]{2,1,0:T(8,128)(2,1)S(1)} %bitcast.3, f32[1024,16]{1,0:T(8,128)S(1)} %copy.5.refs_1_), custom_call_target="tpu_custom_call" | custom-call | tf_op jit(solution)/shard_map/everything/pallas_call | solution.py:369
  92.9 1.3 %copy.9 = f32[512,1024]{1,0:T(8,128)} copy(f32[512,1024]{1,0:T(8,128)S(1)} %get-tuple-element.12) | data formatting | bytes 4194304
  94.3 0.6 copy.10
  94.9 0.6 copy.11
Async XLA Ops:
  1.7 0.9 copy-start

commit v3 on v2

--- a/solution.py
+++ b/solution.py
@@ -33,8 +33,8 @@
 
 def kernel(
     tokens, omega, acts, grads, f_out, ap_out, sol_out,
-    AC, AK, LB, SC, GX, APH, YA, YP, P1, P2, P3, P4, YS, R1, S2, R2, R3, APS, APT,
-    sc_s, sc_r, zl_s, zl_r, x_s, x_r, sib_s, sib_r, zs_s, zs_r, xs_s, p_r, ys_s, ys_r,
+    AC, AK, LB, SC, GR, GX, APH, YA, YP, P1, P2, P3, P4, YS, R1, S2, R2, R3, APS, APT,
+    v_s, sc_s, sc_r, zl_s, zl_r, x_s, x_r, sib_s, sib_r, zs_s, zs_r, xs_s, p_r, ys_s, ys_r,
     gx_s, gx_r, p1_s, p1_r, p2_s, p2_r, ya_s, ya_r, rs_s, rs_r, zh_s, zh_r, ag_s, ag_r, ap_s, ap_r,
 ):
     zl, x, core, y, zh = [lax.axis_index(a) for a in AXES]
@@ -54,6 +54,11 @@
 
     def wait(ref, sem):
         pltpu.make_async_copy(ref, ref, sem).wait()
+
+    own = pltpu.make_async_copy(acts, AC.at[x, zl, :, core], ap_s.at[2])
+    own.start()
+    bring = pltpu.make_async_copy(grads, GR, ap_s.at[3])
+    bring.start()
 
     barrier = pltpu.get_barrier_semaphore()
 
@@ -75,14 +80,13 @@
             if dz and dl:
                 hello(dev(zl_=plus(zl, dl), zh_=plus(zh, dz)))
     mirror = [dev(zl_=y, x_=zh, core_=lax.rem(core + dc, 2), y_=zl, zh_=x) for dc in range(2)]
-    pl.when(jnp.logical_not(diagonal))(lambda: hello(mirror[0]))
-    hello(mirror[1])
-
-    g = jnp.transpose(grads[...])
+
+    own.wait()
+    bring.wait()
+    g = GR[...]
     GX[x] = two_terms(g)
 
-    greeted = 13 + 9 + 3 + 9 + 1
-    pl.semaphore_wait(barrier, greeted + jnp.where(diagonal, 0, 1))
+    pl.semaphore_wait(barrier, 13 + 9 + 3 + 9)
 
     def spot(dx, dl):
         return AC.at[plus(x, 4 - dx), plus(zl, 4 - dl), :, core]
@@ -101,7 +105,7 @@
         for dy in (1, 3, 2, 0):
             for dc in range(2):
                 part, half = plus(y, dy), lax.rem(core + dc, 2)
-                src = acts.at[part, :, pl.ds(pl.multiple_of(half * 512, 512), 512)]
+                src = AC.at[x, zl, part, core, :, pl.ds(pl.multiple_of(half * 512, 512), 512)]
                 dst = SC.at[y, core]
                 if dy or dc:
                     send(src, dst, sc_s, sc_r, dev(core_=half, y_=part))
@@ -116,6 +120,11 @@
                 send(SC.at[at], dst, zs_s.at[0 if dz == 0 else 1], zs_r.at[dz], dev(zl_=at, zh_=plus(zh, dz)))
             else:
                 pltpu.make_async_copy(SC.at[at], dst, zs_r.at[0]).start()
+
+    def relay_z():
+        for d, part in ((1, pl.ds(0, 4)), (3, pl.ds(4, 4))):
+            at = LB.at[plus(zh, 4 - d), part]
+            send(at, at, v_s, zs_r.at[2], dev(zh_=plus(zh, d)))
 
     def pass_on(dz):
         wait(LB.at[0], zs_r.at[dz])
@@ -246,32 +255,29 @@
         lax.fori_loop(0, 4, tile, 0)
 
     scatter()
-    own = pltpu.make_async_copy(acts, spot(0, 0), ap_s.at[2])
-    own.start()
+    mine = spot(0, 0)
     for d in (1, 3, 2):
-        send(acts, spot(0, 0), zl_s, zl_r.at[d - 1], dev(zl_=plus(zl, d)))
-    to_sib(acts, 0, 0)
+        send(mine, mine, zl_s, zl_r.at[d - 1], dev(zl_=plus(zl, d)))
+    to_sib(mine, 0, 0)
     for d in (1, 3, 2):
         send(GX.at[x], GX.at[x], gx_s, gx_r.at[d - 1], dev(x_=plus(x, d)))
-    to_x(acts, 0)
+    to_x(mine, 0)
     for d in (1, 3, 2):
         wait(spot(0, d), zl_r.at[d - 1])
         to_x(spot(0, d), d)
         to_sib(spot(0, d), 0, d)
         if d == 1:
-            own.wait()
             for e in (1, 3, 2):
                 wait(GX.at[0], gx_r.at[e - 1])
             wait(sib_spot(0, 0), sib_r.at[0, 0])
             first_partial(0)
+    wait(SC, sc_r)
+    over_z(1)
+    over_z(3)
     for d in (1, 3, 2):
         wait(sib_spot(0, d), sib_r.at[0, d])
         first_partial(d)
     first_cross()
-    wait(SC, sc_r)
-    over_z(2)
-    over_z(1)
-    over_z(3)
     over_z(0)
     for dl in (0, 1, 3, 2):
         for dx in (1, 3):
@@ -280,10 +286,12 @@
                 send(spot(dx, dl), spot(dx, dl), x_s, x_r.at[1, dl], dev(x_=plus(x, dx)))
             to_sib(spot(dx, dl), dx, dl)
     first_spread()
+    pass_on(1)
+    pass_on(3)
+    relay_z()
     for dl in (0, 1, 3, 2):
         wait(spot(2, dl), x_r.at[1, dl])
         to_sib(spot(2, dl), 2, dl)
-    pass_on(2)
     total = first_collect(0)
     for q in (1, 3, 2):
         sib_quarter(q)
@@ -294,9 +302,8 @@
         APS[h] = applied[:, 512 * h : 512 * (h + 1)]
     for q in (0, 1, 3, 2):
         partial(q)
-    pass_on(1)
-    pass_on(3)
     pass_on(0)
+    pass_on(2)
     for q in (0, 1, 3, 2):
         cross(q)
     for dc in range(2):
@@ -311,9 +318,9 @@
                 send(APS.at[half], APT.at[core], ap_s.at[0], ap_r.at[0], mirror[0])
         else:
             send(APS.at[half], APT.at[core], ap_s.at[1], ap_r.at[1], mirror[1])
-    over_y(2)
     over_y(1)
     over_y(3)
+    over_y(2)
     over_y(0)
     for q in (0, 1, 3, 2):
         spread(q)
@@ -342,7 +349,8 @@
     wait(AC.at[:, :, :, 0], sib_s)
     wait(LB.at[0, 0:7], sc_s)
     wait(LB.at[0, 0:6], zs_s.at[0])
-    wait(LB.at[0:3], zs_s.at[1])
+    wait(LB.at[0:2], zs_s.at[1])
+    wait(LB.at[0], v_s)
     wait(LB.at[0:3], xs_s)
     wait(AK.at[0:3], ys_s)
     wait(GX.at[0:3], gx_s)
@@ -362,6 +370,7 @@
     omega = step_size(16384, tokens)
     dma = pltpu.SemaphoreType.DMA
     vmem = pl.BlockSpec(memory_space=pltpu.VMEM)
+    anywhere = pl.BlockSpec(memory_space=pltpu.HBM)
 
     def body(*refs):
         kernel(tokens, omega, *refs)
@@ -373,13 +382,14 @@
             jax.ShapeDtypeStruct((32, 512), F32),
             jax.ShapeDtypeStruct((16, 1024), F32),
         ),
-        in_specs=[vmem, vmem],
+        in_specs=[anywhere, anywhere],
         out_specs=[vmem, vmem, vmem],
         scratch_shapes=[
             pltpu.VMEM((4, 4, 4, 2, 16, 1024), BF16),
             pltpu.VMEM((4, 4, 8, 16, 512), BF16),
             pltpu.VMEM((4, 8, 16, 512), BF16),
             pltpu.VMEM((4, 2, 16, 512), BF16),
+            pltpu.VMEM((16, 1024), F32),
             pltpu.VMEM((4, 32, 1024), BF16),
             pltpu.VMEM((32, 1024), BF16),
             pltpu.VMEM((4, 4, 16, 128), F32),
@@ -395,17 +405,17 @@
             pltpu.VMEM((4, 4, 16, 128), F32),
             pltpu.VMEM((2, 16, 512), F32),
             pltpu.VMEM((2, 16, 512), F32),
-            dma(()), dma(()), dma(()), dma((3,)), dma(()), dma((3, 4)), dma(()), dma((4, 4)),
+            dma(()), dma(()), dma(()), dma(()), dma((3,)), dma(()), dma((3, 4)), dma(()), dma((4, 4)),
             dma((2,)), dma((4,)), dma(()), dma((4,)), dma(()), dma((3, 4)),
             dma(()), dma((3,)), dma(()), dma((4,)), dma(()), dma((3,)), dma((2,)), dma((4, 4)),
             dma(()), dma((4, 3)), dma(()), dma((4, 3)), dma(()), dma((4, 3)),
-            dma((3,)), dma((2,)),
+            dma((4,)), dma((2,)),
         ],
         compiler_params=pltpu.CompilerParams(
             collective_id=0, has_side_effects=True, vmem_limit_bytes=48 * 2**20
         ),
         name="everything",
-    )(acts.reshape(4, 16, 1024), grads)
+    )(acts.reshape(4, 16, 1024), grads.T)
     return factor, ap.T, sol.T
 
 

time: 96.8 us -> 90.3 us (0.933)
  the two profiles are of different devices: /device:TPU:6 before, /device:TPU:4 now
where the time goes in v3:
time: 90.3 us; the launch traced here: 90.1 us
  Pallas kernels  85.2 us (94%)
  local copies, waits for them, and re-layouts  4.32 us (5%)
    pallas_call x1, Pallas kernels, local(): pl.pallas_call(body, out_shape=(jax.ShapeDtypeStruct((512, 1024), F32), j...  85.2 us
    unnamed x7, local copies, waits for them, and re-layouts  4.32 us

profile of v3, /device:TPU:4, one launch (start us, length us, event | category | flops | bytes accessed | tf_op | source)
XLA Modules:
  0.0 90.1 jit_solution(14858085938656315393)
XLA Ops:
  0.6 0.0 copy-start
  0.6 0.9 copy-done
  1.5 0.0 copy-start.1
  1.5 0.8 copy-done.1
  2.4 85.2 %everything.1 = (f32[512,1024]{1,0:T(8,128)S(1)}, f32[32,512]{1,0:T(8,128)S(1)}, f32[16,1024]{1,0:T(8,128)S(1)}) custom-call(bf16[4,16,1024]{2,1,0:T(8,128)(2,1)S(1)} %bitcast.4, f32[16,1024]{1,0:T(8,128)S(1)} %bitcast.5), custom_call_target="tpu_custom_call" | custom-call | tf_op jit(solution)/shard_map/everything/pallas_call | solution.py:378
  87.5 1.3 %copy.8 = f32[512,1024]{1,0:T(8,128)} copy(f32[512,1024]{1,0:T(8,128)S(1)} %get-tuple-element.12) | data formatting | bytes 4194304
  88.9 0.6 copy.9
  89.5 0.6 copy.10
Async XLA Ops:
  0.6 0.9 %copy-start = (bf16[64,1024]{1,0:T(8,128)(2,1)S(1)}, bf16[64,1024]{1,0:T(8,128)(2,1)}, u32[]{:S(2)}) copy-start(bf16[64,1024]{1,0:T(8,128)(2,1)} %param.2) | copy-start | bytes 393220
  1.5 0.8 copy-start.1

commit v4 on v3

--- a/solution.py
+++ b/solution.py
@@ -77,7 +77,7 @@
     hello(dev(core_=sib))
     for dz in range(4):
         for dl in range(4):
-            if dz and dl:
+            if dz in (1, 3) and dl:
                 hello(dev(zl_=plus(zl, dl), zh_=plus(zh, dz)))
     mirror = [dev(zl_=y, x_=zh, core_=lax.rem(core + dc, 2), y_=zl, zh_=x) for dc in range(2)]
 
@@ -86,7 +86,7 @@
     g = GR[...]
     GX[x] = two_terms(g)
 
-    pl.semaphore_wait(barrier, 13 + 9 + 3 + 9)
+    pl.semaphore_wait(barrier, 13 + 9 + 3 + 6)
 
     def spot(dx, dl):
         return AC.at[plus(x, 4 - dx), plus(zl, 4 - dl), :, core]
@@ -306,6 +306,10 @@
     pass_on(2)
     for q in (0, 1, 3, 2):
         cross(q)
+    over_y(1)
+    over_y(3)
+    over_y(2)
+    over_y(0)
     for dc in range(2):
         half = lax.rem(core + dc, 2)
         if dc == 0:
@@ -318,10 +322,6 @@
                 send(APS.at[half], APT.at[core], ap_s.at[0], ap_r.at[0], mirror[0])
         else:
             send(APS.at[half], APT.at[core], ap_s.at[1], ap_r.at[1], mirror[1])
-    over_y(1)
-    over_y(3)
-    over_y(2)
-    over_y(0)
     for q in (0, 1, 3, 2):
         spread(q)
     relay_y()

time: 90.3 us -> 90.3 us (level)
  the two profiles are of different devices: /device:TPU:4 before, /device:TPU:6 now
where the time goes in v4:
time: 90.3 us; the launch traced here: 90.1 us
  Pallas kernels  85.2 us (94%)
  local copies, waits for them, and re-layouts  4.32 us (5%)
    pallas_call x1, Pallas kernels, local(): pl.pallas_call(body, out_shape=(jax.ShapeDtypeStruct((512, 1024), F32), j...  85.2 us
    unnamed x7, local copies, waits for them, and re-layouts  4.32 us

profile of v4, /device:TPU:6, one launch (start us, length us, event | category | flops | bytes accessed | tf_op | source)
XLA Modules:
  0.0 90.1 jit_solution(10517849250245332968)
XLA Ops:
  0.6 0.0 copy-start
  0.6 0.9 copy-done
  1.5 0.0 copy-start.1
  1.5 0.8 copy-done.1
  2.4 85.2 %everything.1 = (f32[512,1024]{1,0:T(8,128)S(1)}, f32[32,512]{1,0:T(8,128)S(1)}, f32[16,1024]{1,0:T(8,128)S(1)}) custom-call(bf16[4,16,1024]{2,1,0:T(8,128)(2,1)S(1)} %bitcast.4, f32[16,1024]{1,0:T(8,128)S(1)} %bitcast.5), custom_call_target="tpu_custom_call" | custom-call | tf_op jit(solution)/shard_map/everything/pallas_call | solution.py:378
  87.6 1.3 %copy.8 = f32[512,1024]{1,0:T(8,128)} copy(f32[512,1024]{1,0:T(8,128)S(1)} %get-tuple-element.12) | data formatting | bytes 4194304
  88.9 0.6 copy.9
  89.5 0.6 copy.10
Async XLA Ops:
  0.6 0.9 %copy-start = (bf16[64,1024]{1,0:T(8,128)(2,1)S(1)}, bf16[64,1024]{1,0:T(8,128)(2,1)}, u32[]{:S(2)}) copy-start(bf16[64,1024]{1,0:T(8,128)(2,1)} %param.2) | copy-start | bytes 393220
  1.5 0.8 copy-start.1

commit v5 on v4

--- a/solution.py
+++ b/solution.py
@@ -334,15 +334,16 @@
         + (omega**3 * DAMPING - 3.0 * omega**2) * applied
         + (omega**3 / tokens) * total
     )
-    wait(APT.at[0], ap_r.at[0])
-    wait(APT.at[0], ap_r.at[1])
-    ap_out[...] = APT[...].reshape(32, 512)
     for n in (1, 3, 2):
         for k in range(4):
             if n != 2 and (n == 1) == (k < 2):
                 continue
             wait_y(n, k)
         factor_part(n)
+
+    wait(APT.at[0], ap_r.at[0])
+    wait(APT.at[0], ap_r.at[1])
+    ap_out[...] = APT[...].reshape(32, 512)
 
     wait(AC.at[0:3, 0, :, 0], zl_s)
     wait(AC.at[0:3, :, :, 0], x_s)

time: 90.3 us -> 90.3 us (level)
  no operation moved by 1% of the time
where the time goes in v5:
time: 90.3 us; the launch traced here: 90.1 us
  Pallas kernels  85.2 us (94%)
  local copies, waits for them, and re-layouts  4.32 us (5%)
    pallas_call x1, Pallas kernels, local(): pl.pallas_call(body, out_shape=(jax.ShapeDtypeStruct((512, 1024), F32), j...  85.2 us
    unnamed x7, local copies, waits for them, and re-layouts  4.32 us

profile of v5, /device:TPU:6, one launch (start us, length us, event | category | flops | bytes accessed | tf_op | source)
XLA Modules:
  0.0 90.1 jit_solution(17702774705170879519)
XLA Ops:
  0.6 0.0 copy-start
  0.6 0.9 copy-done
  1.5 0.0 copy-start.1
  1.5 0.8 copy-done.1
  2.4 85.2 %everything.1 = (f32[512,1024]{1,0:T(8,128)S(1)}, f32[32,512]{1,0:T(8,128)S(1)}, f32[16,1024]{1,0:T(8,128)S(1)}) custom-call(bf16[4,16,1024]{2,1,0:T(8,128)(2,1)S(1)} %bitcast.4, f32[16,1024]{1,0:T(8,128)S(1)} %bitcast.5), custom_call_target="tpu_custom_call" | custom-call | tf_op jit(solution)/shard_map/everything/pallas_call | solution.py:379
  87.6 1.3 %copy.8 = f32[512,1024]{1,0:T(8,128)} copy(f32[512,1024]{1,0:T(8,128)S(1)} %get-tuple-element.12) | data formatting | bytes 4194304
  88.9 0.6 copy.9
  89.5 0.6 copy.10
Async XLA Ops:
  0.6 0.9 %copy-start = (bf16[64,1024]{1,0:T(8,128)(2,1)S(1)}, bf16[64,1024]{1,0:T(8,128)(2,1)}, u32[]{:S(2)}) copy-start(bf16[64,1024]{1,0:T(8,128)(2,1)} %param.2) | copy-start | bytes 393220
  1.5 0.8 copy-start.1
